TPU v7x, 512 devices: a whole 4x4x16 slice. The times are simulated.
512 devices in a mesh: tok: 32 (over y, x, core), proto: 16 (over z).
Axes of the slice: x: 4, y: 4, z: 16, core: 2. Of those that a mesh axis runs over, the one named last changes fastest.
Arguments:
- patches: bfloat16 [32768, 256], P(('tok', 'proto'))
- mask_index: int32 [16384], P('tok'), may hold values from 0 to 32767, as said below
- proto_weight: float32 [256, 65536], P('tok', 'proto')
Outputs:
- targets: bfloat16 [16384, 65536], P('tok', 'proto')
Inputs may be any that keep to these rules, and one draw needn't show every extreme that they name: mask_index holds distinct values; the value at position i lies in [(i // 512) * 1024, (i // 512 + 1) * 1024).
All inputs are finite; a program needn't handle non-finite values.
Results may differ from a plain program's by a relative error of at most 0.0072.
Values may be sent and summed in bfloat16 or wider, within the bound.
A program may use at most 64 MiB of HBM per device.

v0:
```python
import jax
import jax.numpy as jnp
from jax import lax
from jax.sharding import PartitionSpec as P

K = 65536
ITERS = 3


teacher_temp = 0.04


def column_total(values):
    return lax.psum(values, "tok")


def row_total(values):
    return lax.psum(values, "proto")


def body(patches, mask_index, proto_weight):
    gathered_rows = lax.all_gather(patches, "proto", axis=0, tiled=True)
    offset = lax.axis_index("tok") * gathered_rows.shape[0]
    local_index = mask_index - offset
    selected = jnp.take(gathered_rows, local_index, axis=0).astype(jnp.float32)
    features = (
        selected * lax.rsqrt(jnp.sum(selected * selected, axis=1, keepdims=True) + 1e-06)
    ).astype(jnp.bfloat16)
    whole = lax.all_gather(proto_weight, "tok", axis=0, tiled=True)
    normed = (whole * lax.rsqrt(jnp.sum(whole * whole, axis=0, keepdims=True) + 1e-06)).astype(
        jnp.bfloat16
    )
    scores = jnp.dot(features, normed, preferred_element_type=jnp.float32)
    exponent = jnp.exp(scores / teacher_temp)
    balanced = exponent
    for step in range(ITERS):
        balanced = balanced / column_total(jnp.sum(balanced, axis=0))[None, :]
        balanced = balanced / row_total(jnp.sum(balanced, axis=1))[:, None]
    targets = K * balanced
    return targets.astype(jnp.bfloat16)


def solution(mesh):
    return jax.shard_map(
        body,
        mesh=mesh,
        in_specs=(P(("tok", "proto"), None), P("tok"), P("tok", "proto")),
        out_specs=P("tok", "proto"),
        check_vma=False,
    )
```

profile of v0, /device:TPU:1, one launch (start us, length us, event | category | flops | bytes accessed | tf_op | source)
XLA Modules:
  0.0 571.9 jit_solution(6655687228491682287)
XLA Ops:
  6.5 0.0 all-gather.2.cloned.1.call-start
  6.5 0.7 all-gather.2.cloned.1.call-update
  7.3 0.7 compare_and_fusion
  8.0 32.1 %all_gather.6 = bf16[1024,256]{1,0:T(8,128)(2,1)S(1)} all-gather(bf16[64,256]{1,0:T(8,128)(2,1)} %param.3), channel_id=1, replica_groups=mesh['tok'=32,'proto'=16] {'proto'}, dimensions={0}, use_global_device_ids=true | all-gather | bytes 557056 | tf_op jit(solution)/shard_map/all_gather | solution.py:22
  40.0 1.9 gather_fusion
  42.0 0.2 fusion.14
  42.2 35.4 %all-gather.2.cloned.1.call-done = f32[256,4096]{1,0:T(8,128)} async-done(((f32[8,4096]{1,0:T(8,128)}), f32[256,4096]{1,0:T(8,128)}) %all-gather.2.cloned.1.call-update) | async-done | bytes 4194320 | tf_op jit(solution)/shard_map/all_gather | solution.py:29
  77.6 2.5 multiply_reduce_fusion
  80.2 6.6 %fusion.19 = (f32[4096]{0:T(1024)S(1)}, f32[512,4096]{1,0:T(8,128)}) fusion(f32[256,4096]{1,0:T(8,128)} %all-gather.2.cloned.1.call-done, f32[4096]{0:T(1024)S(1)} %add_rsqrt_fusion, f32[512]{0:T(512)S(1)} %add_rsqrt_fusion.1, bf16[512,256]{1,0:T(8,128)(2,1)S(1)} %gather_fusion, pred[512]{0:T(512)(128)(4,1)S(1)} %get-tuple-element.5), kind=kOutput, calls=%fused_computation.33 | convolution fusion | flops 1080553472 | bytes 12880384 | tf_op jit(solution)/shard_map/dot_general | solution.py:33
  86.7 120.9 %psum.42 = f32[4096]{0:T(1024)S(1)} all-reduce(f32[4096]{0:T(1024)S(1)} %get-tuple-element.7), channel_id=1, replica_groups=mesh['tok'=32,'proto'=16] {'tok'}, use_global_device_ids=true, to_apply=%region_3.4 | all-reduce | flops 4096 | bytes 32768 | tf_op jit(solution)/shard_map/psum | solution.py:14
  207.6 4.0 divide_reduce_fusion
  211.6 24.1 %psum.43 = f32[512]{0:T(512)S(1)} all-reduce(f32[512]{0:T(512)S(1)} %divide_reduce_fusion), channel_id=1, replica_groups=mesh['tok'=32,'proto'=16] {'proto'}, use_global_device_ids=true, to_apply=%region_5.6 | all-reduce | flops 512 | bytes 4096 | tf_op jit(solution)/shard_map/psum | solution.py:18
  235.7 4.7 fusion.8
  240.4 131.0 %psum.44 = f32[4096]{0:T(1024)S(1)} all-reduce(f32[4096]{0:T(1024)S(1)} %fusion.8), channel_id=1, replica_groups=mesh['tok'=32,'proto'=16] {'tok'}, use_global_device_ids=true, to_apply=%region_7.8 | all-reduce | flops 4096 | bytes 32768 | tf_op jit(solution)/shard_map/psum | solution.py:14
  371.4 4.3 fusion.10
  375.7 21.1 %psum.45 = f32[512]{0:T(512)S(1)} all-reduce(f32[512]{0:T(512)S(1)} %fusion.10), channel_id=1, replica_groups=mesh['tok'=32,'proto'=16] {'proto'}, use_global_device_ids=true, to_apply=%region_9.10 | all-reduce | flops 512 | bytes 4096 | tf_op jit(solution)/shard_map/psum | solution.py:18
  396.9 4.5 fusion.11
  401.3 131.0 %psum.46 = f32[4096]{0:T(1024)S(1)} all-reduce(f32[4096]{0:T(1024)S(1)} %fusion.11), channel_id=1, replica_groups=mesh['tok'=32,'proto'=16] {'tok'}, use_global_device_ids=true, to_apply=%region_11.12 | all-reduce | flops 4096 | bytes 32768 | tf_op jit(solution)/shard_map/psum | solution.py:14
  532.3 4.6 fusion.12
  537.0 21.7 %psum.47 = f32[512]{0:T(512)S(1)} all-reduce(f32[512]{0:T(512)S(1)} %fusion.12), channel_id=1, replica_groups=mesh['tok'=32,'proto'=16] {'proto'}, use_global_device_ids=true, to_apply=%region_13.14 | all-reduce | flops 512 | bytes 4096 | tf_op jit(solution)/shard_map/psum | solution.py:18
  558.6 6.4 %fusion.9 = bf16[512,4096]{1,0:T(8,128)(2,1)} fusion(f32[512,4096]{1,0:T(8,128)} %get-tuple-element.8, f32[512]{0:T(512)S(1)} %psum.47, f32[4096]{0:T(1024)S(1)} %psum.46, f32[512]{0:T(512)S(1)} %psum.45, f32[4096]{0:T(1024)S(1)} %psum.44, f32[512]{0:T(512)S(1)} %psum.43, f32[4096]{0:T(1024)S(1)} %psum.42), kind=kLoop, calls=%fused_computation.14 | loop fusion | flops 16777216 | bytes 12638208 | tf_op jit(solution)/shard_map/convert_element_type | solution.py:40
  (3 shorter events, 0.0 us)
Async XLA Ops:
  6.5 71.1 %all-gather.2.cloned.1.call-start = ((), (), s32[]{:S(2)}) async-start(), calls=%async_computation | async-start | bytes 4325376 | tf_op jit(solution)/shard_map/all_gather | solution.py:29
Sparse Core Ops, SparseCore 0:
  10.5 67.0 all-gather.1
where the time goes:
time: 582 us; the launch traced here: 572 us
  blocking collectives  482 us (83%)
  waiting for transfers between devices  36.1 us (6%)
  other arithmetic  32 us (5%)
  between operations  13.4 us (2%)
  matrix products  6.56 us (1%)
    psum x3, blocking collectives, column_total(): return lax.psum(values, 'tok')  383 us
    psum x3, blocking collectives, row_total(): return lax.psum(values, 'proto')  66.9 us
    all_gather x1, waiting for transfers between devices, body(): whole = lax.all_gather(proto_weight, 'tok', axis=0, tiled=True)  35.4 us
    all_gather x1, blocking collectives, body(): gathered_rows = lax.all_gather(patches, 'proto', axis=0, tiled=True)  32.1 us
    reduce_sum x3, other arithmetic, body(): balanced = balanced / row_total(jnp.sum(balanced, axis=1))[:, None]  12.9 us
  transfers between devices with their start and end apart: 1, of which 1 were waited for; matrix products, arithmetic and copies ran while one was open for 1% of the time, Pallas kernels for 0%

commit v1 on v0

v1 whole, which is shorter than its diff:
```python
import functools
import math

import jax
import jax.numpy as jnp
from jax import lax
from jax.experimental import pallas as pl
from jax.experimental.pallas import tpu as pltpu
from jax.sharding import PartitionSpec as P

ITERS = 3
EPS = 1e-06
TEMP = 0.04
MESH = pl.DeviceIdType.MESH
F32 = jnp.float32
BF16 = jnp.bfloat16


def far_first(n):
    return sorted(range(1, n), key=lambda d: -min(d, n - d))


def kernel(
    side, depth,
    patches_hbm, index_hbm, weight_hbm,
    expo, row_bcast, col_scale,
    patches_ref, index_ref, weight_ref,
    gathered, onehot, features, wrows, ss_own, ss_a, ss_y, normed,
    row_acc, col_a, col_b, row_x,
    load_sem, ring_send, ring_recv, w_send, w_recv, ss_send, ss_recv,
    n1_send, n1_recv, n2_send, n2_recv, share_send, share_recv,
    a_send, a_recv, b_send, b_recv, r_send, r_recv,
):
    t = lax.axis_index("tok")
    z = lax.axis_index("proto")
    core = lax.rem(t, 2)
    chip = t // 2
    x = lax.rem(chip, side)
    y = chip // side
    q = lax.rem(t, 2 * side)
    sibling = (t + 1 - 2 * core, z)
    tokens, columns = expo.shape
    half = columns // 2
    group = columns // 8
    part = half // 8
    block, width = patches_ref.shape

    def at_z(d):
        return (t, lax.rem(z + d, depth))

    def at_q(d):
        return (y * (2 * side) + lax.rem(q + d, 2 * side), z)

    def at_x(d):
        return ((y * side + lax.rem(x + d, side)) * 2 + core, z)

    def at_y(d):
        return (lax.rem(y + d, side) * (2 * side) + q, z)

    def push(src, dst, send, recv, device):
        copy = pltpu.make_async_remote_copy(
            src_ref=src, dst_ref=dst, send_sem=send, recv_sem=recv,
            device_id=device, device_id_type=MESH,
        )
        copy.start()
        return copy

    def arrived(ref, sem):
        pltpu.make_async_copy(ref, ref, sem).wait()

    def exchange(buf, n, device, send, recv):
        for d in far_first(n):
            push(buf.at[0], buf.at[d], send, recv, device(d))

    def settle(buf, n, recv):
        arrived(buf.at[pl.ds(1, n - 1)], recv)

    barrier = pltpu.get_barrier_semaphore()
    partners = (
        [at_z(1), at_z(depth - 1)]
        + [at_q(d) for d in range(1, 2 * side)]
        + [at_y(d) for d in range(1, side)]
    )
    for device in partners:
        pl.semaphore_signal(barrier, inc=1, device_id=device, device_id_type=MESH)

    loads = [
        pltpu.make_async_copy(src, dst, load_sem.at[i])
        for i, (src, dst) in enumerate((
            (weight_hbm, weight_ref), (patches_hbm, patches_ref), (index_hbm, index_ref)))
    ]
    for load in loads:
        load.start()

    loads[0].wait()
    square = jnp.sum(weight_ref[...] * weight_ref[...], axis=0, keepdims=True)
    for h in range(2):
        for k in range(8):
            lane = h * half + k * part
            ss_own[h, k:k + 1, :] = square[:, lane:lane + part]
    ss_a[0] = ss_own[core]
    own_half = pl.ds(pl.multiple_of(core * half, half), half)
    other_half = pl.ds(pl.multiple_of((1 - core) * half, half), half)
    wrows[core] = weight_ref[:, own_half]

    loads[1].wait()
    loads[2].wait()
    rows = patches_ref[...].astype(F32)
    norm = lax.rsqrt(jnp.sum(rows * rows, axis=1, keepdims=True) + EPS)
    own = pl.ds(pl.multiple_of(z * block, block), block)
    gathered[own, :] = (rows * norm).astype(BF16)

    pl.semaphore_wait(barrier, len(partners))

    for d in far_first(2 * side):
        push(ss_own.at[lax.rem(q + d, 2)], ss_a.at[d], ss_send.at[0], ss_recv.at[0], at_q(d))

    right_steps, left_steps = depth // 2, depth // 2 - 1

    def ring_slot(owner):
        owner = lax.rem(owner + depth, depth)
        return gathered.at[pl.ds(pl.multiple_of(owner * block, block), block)]

    def ring_step(s):
        if s < right_steps:
            if s >= 1:
                arrived(ring_slot(z - s), ring_recv.at[0, s - 1])
            push(ring_slot(z - s), ring_slot(z - s), ring_send.at[0, s],
                 ring_recv.at[0, s], at_z(1))
        if s < left_steps:
            if s >= 1:
                arrived(ring_slot(z + s), ring_recv.at[1, s - 1])
            push(ring_slot(z + s), ring_slot(z + s), ring_send.at[1, s],
                 ring_recv.at[1, s], at_z(depth - 1))

    ring_step(0)

    push(weight_ref.at[:, other_half], wrows.at[core], w_send, w_recv, sibling)

    for j in range(tokens // 128):
        local = (index_ref[j:j + 1, :] - t * (block * depth)).astype(F32)
        column = jnp.broadcast_to(local, (128, 128)).T
        for k in range(block * depth // 128):
            lane = lax.broadcasted_iota(jnp.int32, (128, 128), 1).astype(F32) + 128 * k
            onehot[128 * j:128 * (j + 1), 128 * k:128 * (k + 1)] = jnp.where(
                column == lane, 1.0, 0.0).astype(BF16)

    ring_step(1)
    settle(ss_a, 2 * side, ss_recv.at[0])
    ss_y[0] = jnp.sum(ss_a[...], axis=0)
    exchange(ss_y, side, at_y, ss_send.at[1], ss_recv.at[1])
    ring_step(2)
    ring_step(3)
    arrived(wrows.at[1 - core], w_recv)
    settle(ss_y, side, ss_recv.at[1])
    inverse = lax.rsqrt(jnp.sum(ss_y[...], axis=0) + EPS)
    for k in range(8):
        value = wrows[:, :, k * part:(k + 1) * part].reshape(2 * wrows.shape[1], part)
        lane = (k % 2) * part
        normed[core, k // 4, (k // 2) % 2, y, x, :, lane:lane + part] = (
            value * inverse[k:k + 1, :]).astype(BF16)

    gather = []
    for d in far_first(side):
        gather.append(push(normed.at[core, 0, :, y, x], normed.at[core, 0, :, y, x],
                           n1_send.at[0, d], n1_recv.at[0, d], at_x(d)))
        gather.append(push(normed.at[core, 1, :, y, x], normed.at[core, 1, :, y, x],
                           n1_send.at[1, d], n1_recv.at[1, d], at_y(d)))
    ring_step(4)
    ring_step(5)
    for d in range(1, side):
        px, py = lax.rem(x - d + side, side), lax.rem(y - d + side, side)
        arrived(normed.at[core, 0, :, y, px], n1_recv.at[0, d])
        arrived(normed.at[core, 1, :, py, x], n1_recv.at[1, d])
    for c in range(2):
        for d in far_first(side):
            gather.append(push(normed.at[core, 0, c, y], normed.at[core, 0, c, y],
                               n2_send.at[0, c, d], n2_recv.at[0, c, d], at_y(d)))
            gather.append(push(normed.at[core, 1, c, :, x], normed.at[core, 1, c, :, x],
                               n2_send.at[1, c, d], n2_recv.at[1, c, d], at_x(d)))
    for s in range(6, right_steps):
        ring_step(s)
    arrived(ring_slot(z - right_steps), ring_recv.at[0, right_steps - 1])
    arrived(ring_slot(z + left_steps), ring_recv.at[1, left_steps - 1])
    features[...] = jnp.dot(onehot[...], gathered[...],
                            preferred_element_type=F32).astype(BF16)

    factor = math.log2(math.e) / TEMP
    step_lanes = min(256, group)

    def fill(which, c):
        def chunk(i, carry):
            p = i // (group // step_lanes)
            start = pl.multiple_of(lax.rem(i, group // step_lanes) * step_lanes, step_lanes)
            lanes = pl.ds(start, step_lanes)
            weights = normed[which, p, c, :, :, :, lanes].reshape(width, step_lanes)
            row = which * 4 + p * 2 + c
            target = pl.ds(pl.multiple_of(row * group + start, step_lanes), step_lanes)
            scores = jnp.dot(features[...], weights, preferred_element_type=F32)
            value = jnp.exp2(scores * factor)
            expo[:, target] = value
            total = jnp.sum(value.reshape(tokens // 8, 8, step_lanes), axis=0)
            col_a[0, 0, pl.ds(row, 1), lanes] = jnp.sum(total, axis=0, keepdims=True)
            return carry

        lax.fori_loop(0, 2 * (group // step_lanes), chunk, 0)

    for c in range(2):
        for d in range(1, side):
            px, py = lax.rem(x - d + side, side), lax.rem(y - d + side, side)
            arrived(normed.at[core, 0, c, py], n2_recv.at[0, c, d])
            arrived(normed.at[core, 1, c, :, px], n2_recv.at[1, c, d])
        gather.append(push(normed.at[core, :, c], normed.at[core, :, c],
                           share_send.at[c], share_recv.at[c], sibling))
        fill(core, c)
    for c in range(2):
        arrived(normed.at[1 - core, :, c], share_recv.at[c])
        fill(1 - core, c)

    def columns_to_scale(it):
        exchange(col_a.at[it], 2 * side, at_q, a_send.at[it], a_recv.at[it])
        settle(col_a.at[it], 2 * side, a_recv.at[it])
        col_b[it, 0] = jnp.sum(col_a[it], axis=0)
        exchange(col_b.at[it], side, at_y, b_send.at[it], b_recv.at[it])
        settle(col_b.at[it], side, b_recv.at[it])
        col_scale[...] = 1.0 / jnp.sum(col_b[it], axis=0)

    def row_pass(it):
        def some(g, carry):
            here = pl.ds(pl.multiple_of(g * 64, 64), 64)
            total = jnp.zeros((64, 128), F32)
            for j in range(columns // 128):
                k, l = j // (group // 128), j % (group // 128)
                scale = col_scale[k:k + 1, 128 * l:128 * (l + 1)]
                total += expo[here, 128 * j:128 * (j + 1)] * scale
            row_acc[here, :] = total
            return carry

        lax.fori_loop(0, tokens // 64, some, 0)
        for j in range(tokens // 128):
            turned = row_acc[128 * j:128 * (j + 1), :].T
            row_x[it, 0, j:j + 1, :] = jnp.sum(turned, axis=0, keepdims=True)

    def rows_to_scale(it):
        exchange(row_x.at[it], depth, at_z, r_send.at[it], r_recv.at[it])
        settle(row_x.at[it], depth, r_recv.at[it])
        scale = 1.0 / jnp.sum(row_x[it], axis=0)
        for j in range(tokens // 128):
            row_bcast[128 * j:128 * (j + 1), :] = jnp.broadcast_to(
                scale[j:j + 1, :], (128, 128)).T

    def column_pass(it):
        def chunk(k, carry):
            target = pl.ds(pl.multiple_of(k * group, group), group)

            total = jnp.zeros((8, group), F32)
            for g in range(tokens // 64):
                here = slice(g * 64, (g + 1) * 64)
                scale = jnp.concatenate([row_bcast[here, :]] * (group // 128), axis=1)
                value = expo[here, target] * scale
                total += jnp.sum(value.reshape(8, 8, group), axis=0)
            col_a[it, 0, pl.ds(k, 1), :] = jnp.sum(total, axis=0, keepdims=True)
            return carry

        lax.fori_loop(0, 8, chunk, 0)

    def sinkhorn(it, carry):
        columns_to_scale(it)
        row_pass(it)
        rows_to_scale(it)
        column_pass(it + 1)
        return carry

    lax.fori_loop(0, ITERS - 1, sinkhorn, 0)
    columns_to_scale(ITERS - 1)
    row_pass(ITERS - 1)
    rows_to_scale(ITERS - 1)

    pltpu.make_async_copy(wrows.at[core], wrows.at[core], w_send).wait()
    for s in range(right_steps):
        arrived(ring_slot(z - s), ring_send.at[0, s])
    for s in range(left_steps):
        arrived(ring_slot(z + s), ring_send.at[1, s])
    for copy in gather:
        copy.wait_send()
    settle(ss_a, 2 * side, ss_send.at[0])
    settle(ss_y, side, ss_send.at[1])
    for it in range(ITERS):
        settle(col_a.at[it], 2 * side, a_send.at[it])
        settle(col_b.at[it], side, b_send.at[it])
        settle(row_x.at[it], depth, r_send.at[it])


def finish_kernel(scale_out, expo, row_bcast, col_scale, out_ref, staged, sems):
    tokens, columns = expo.shape
    group = columns // 8
    step = staged.shape[1]
    copies = []
    for g in range(tokens // step):
        here = slice(g * step, (g + 1) * step)
        scale = jnp.concatenate([row_bcast[here, :]] * (group // 128), axis=1)
        for k in range(8):
            target = slice(k * group, (k + 1) * group)
            value = scale_out * (expo[here, target] * scale)
            staged[g, :, target] = (value * col_scale[k:k + 1, :]).astype(BF16)
        copies.append(pltpu.make_async_copy(staged.at[g], out_ref.at[pl.ds(g * step, step)],
                                            sems.at[g]))
        copies[-1].start()
    for copy in copies:
        copy.wait()


def body(side, depth, patches, mask_index, proto_weight):
    block, width = patches.shape
    tokens = mask_index.shape[0]
    rows, columns = proto_weight.shape
    half, group = columns // 2, columns // 8
    dma = pltpu.SemaphoreType.DMA
    vmem = pl.BlockSpec(memory_space=pltpu.VMEM)
    hbm = pl.BlockSpec(memory_space=pltpu.HBM)
    expo, row_bcast, col_scale = pl.pallas_call(
        functools.partial(kernel, side, depth),
        out_shape=(
            jax.ShapeDtypeStruct((tokens, columns), F32),
            jax.ShapeDtypeStruct((tokens, 128), F32),
            jax.ShapeDtypeStruct((8, group), F32),
        ),
        in_specs=[hbm] * 3,
        out_specs=(vmem,) * 3,
        scratch_shapes=[
            pltpu.VMEM((block, width), BF16),
            pltpu.VMEM((tokens // 128, 128), jnp.int32),
            pltpu.VMEM((rows, columns), F32),
            pltpu.VMEM((block * depth, width), BF16),
            pltpu.VMEM((tokens, block * depth), BF16),
            pltpu.VMEM((tokens, width), BF16),
            pltpu.VMEM((2, rows, half), F32),
            pltpu.VMEM((2, 8, half // 8), F32),
            pltpu.VMEM((2 * side, 8, half // 8), F32),
            pltpu.VMEM((side, 8, half // 8), F32),
            pltpu.VMEM((2, 2, 2, side, side, 2 * rows, group), BF16),
            pltpu.VMEM((tokens, 128), F32),
            pltpu.VMEM((ITERS, 2 * side, 8, group), F32),
            pltpu.VMEM((ITERS, side, 8, group), F32),
            pltpu.VMEM((ITERS, depth, tokens // 128, 128), F32),
            dma((3,)),
            dma((2, depth // 2)), dma((2, depth // 2)),
            dma, dma,
            dma((2,)), dma((2,)),
            dma((2, side)), dma((2, side)),
            dma((2, 2, side)), dma((2, 2, side)),
            dma((2,)), dma((2,)),
            dma((ITERS,)), dma((ITERS,)),
            dma((ITERS,)), dma((ITERS,)),
            dma((ITERS,)), dma((ITERS,)),
        ],
        compiler_params=pltpu.CompilerParams(
            collective_id=0, has_side_effects=True,
            vmem_limit_bytes=32 * 1024 * 1024,
        ),
        cost_estimate=pl.CostEstimate(
            flops=2 * tokens * columns * width, bytes_accessed=4 * tokens * columns,
            transcendentals=tokens * columns),
    )(*(pltpu.with_memory_space_constraint(v, pltpu.HBM) for v in (
        patches, mask_index.reshape(tokens // 128, 128), proto_weight)))
    step = 64
    return pl.pallas_call(
        functools.partial(finish_kernel, float(columns * depth)),
        out_shape=jax.ShapeDtypeStruct((tokens, columns), BF16),
        in_specs=[vmem] * 3,
        out_specs=hbm,
        scratch_shapes=[pltpu.VMEM((tokens // step, step, columns), BF16),
                        dma((tokens // step,))],
        compiler_params=pltpu.CompilerParams(vmem_limit_bytes=16 * 1024 * 1024),
        cost_estimate=pl.CostEstimate(
            flops=3 * tokens * columns, bytes_accessed=6 * tokens * columns, transcendentals=0),
    )(expo, row_bcast, col_scale)


def solution(mesh):
    side = math.isqrt(mesh.shape["tok"] // 2)
    return jax.shard_map(
        functools.partial(body, side, mesh.shape["proto"]),
        mesh=mesh,
        in_specs=(P(("tok", "proto"), None), P("tok"), P("tok", "proto")),
        out_specs=P("tok", "proto"),
        check_vma=False,
    )
```

time: 582 us -> 92.1 us (0.16); the launches traced: 572 us -> 91.8 us
  blocking collectives: 482 us -> 0 us
  Pallas kernels: 0 us -> 91.8 us
  waiting for transfers between devices: 36.1 us -> 0 us
  other arithmetic: 32 us -> 0 us
  between operations: 13.4 us -> 0.01 us
  matrix products: 6.56 us -> 0 us
    psum x6 -> x0, blocking collectives: 450 us -> none  [the longest x3 383 us: column_total(): return lax.psum(values, 'tok')]
    pallas_call x0 -> x2, Pallas kernels: none -> 91.8 us  [the longest x1 89.6 us: body(): pl.pallas_call(functools.partial(kernel, side, depth), out_shape=(jax.Sha...]
    all_gather x1 -> x0, waiting for transfers between devices: 35.4 us -> none  [body(): whole = lax.all_gather(proto_weight, 'tok', axis=0, tiled=True)]
    all_gather x1 -> x0, blocking collectives: 32.1 us -> none  [body(): gathered_rows = lax.all_gather(patches, 'proto', axis=0, tiled=True)]
    reduce_sum x7 -> x0, other arithmetic: 24.9 us -> none  [the longest x3 12.9 us: body(): balanced = balanced / row_total(jnp.sum(balanced, axis=1))[:, None]]
    dot_general x1 -> x0, matrix products: 6.56 us -> none  [body(): scores = jnp.dot(features, normed, preferred_element_type=jnp.float32)]
    convert_element_type x1 -> x0, other arithmetic: 6.43 us -> none  [body(): return targets.astype(jnp.bfloat16)]
  transfers between devices with their start and end apart: 1 -> 0, of which waited for: 1 -> 0; matrix products, arithmetic and copies ran while one was open for 1% -> 0% of each run, Pallas kernels for 0% -> 0%
where the time goes in v1:
time: 92.1 us; the launch traced here: 91.8 us
  Pallas kernels  91.8 us (100%)
    pallas_call x1, Pallas kernels, body(): pl.pallas_call(functools.partial(kernel, side, depth), out_shape=(jax.Sha...  89.6 us
    pallas_call x1, Pallas kernels, body(): pl.pallas_call(functools.partial(finish_kernel, float(columns * depth)),...  2.19 us

profile of v1, /device:TPU:1, one launch (start us, length us, event | category | flops | bytes accessed | tf_op | source)
XLA Modules:
  0.0 91.8 jit_solution(6070173746565739816)
XLA Ops:
  0.0 89.6 %shard_map.37 = (f32[512,4096]{1,0:T(8,128)S(1)}, f32[512,128]{1,0:T(8,128)S(1)}, f32[8,512]{1,0:T(8,128)S(1)}) custom-call(bf16[64,256]{1,0:T(8,128)(2,1)} %patches_hbm.1, s32[4,128]{1,0:T(4,128)} %bitcast.1, f32[8,4096]{1,0:T(8,128)} %weight_hbm.1), custom_call_target="tpu_custom_call" | custom-call | flops 1073741824 | bytes 8388608 | tf_op jit(solution)/shard_map/pallas_call | solution.py:321
  89.6 2.2 %shard_map.38 = bf16[512,4096]{1,0:T(8,128)(2,1)} custom-call(f32[512,4096]{1,0:T(8,128)S(1)} %get-tuple-element.8.expo, f32[512,128]{1,0:T(8,128)S(1)} %get-tuple-element.9.row_bcast, f32[8,512]{1,0:T(8,128)S(1)} %get-tuple-element.10.col_scale), custom_call_target="tpu_custom_call" | custom-call | flops 6291456 | bytes 12582912 | tf_op jit(solution)/shard_map/pallas_call | solution.py:367

commit v2 on v1

--- a/solution.py
+++ b/solution.py
@@ -51,6 +51,10 @@
     def at_q(d):
         return (y * (2 * side) + lax.rem(q + d, 2 * side), z)
 
+    def at_qy(d):
+        to = lax.rem(y * 2 + core + d, 2 * side)
+        return ((to // 2) * (2 * side) + x * 2 + lax.rem(to, 2), z)
+
     def at_x(d):
         return ((y * side + lax.rem(x + d, side)) * 2 + core, z)
 
@@ -77,9 +81,9 @@
 
     barrier = pltpu.get_barrier_semaphore()
     partners = (
-        [at_z(1), at_z(depth - 1)]
+        [at_z(1), at_z(2), at_z(depth - 1), at_z(depth - 2)]
         + [at_q(d) for d in range(1, 2 * side)]
-        + [at_y(d) for d in range(1, side)]
+        + [at_qy(d) for d in range(1, 2 * side)]
     )
     for device in partners:
         pl.semaphore_signal(barrier, inc=1, device_id=device, device_id_type=MESH)
@@ -115,23 +119,30 @@
     for d in far_first(2 * side):
         push(ss_own.at[lax.rem(q + d, 2)], ss_a.at[d], ss_send.at[0], ss_recv.at[0], at_q(d))
 
-    right_steps, left_steps = depth // 2, depth // 2 - 1
-
-    def ring_slot(owner):
-        owner = lax.rem(owner + depth, depth)
+    reach = (depth // 2, depth - 1 - depth // 2)
+
+    def ring_slot(way, d):
+        owner = lax.rem(z - d + depth, depth) if way == 0 else lax.rem(z + d, depth)
         return gathered.at[pl.ds(pl.multiple_of(owner * block, block), block)]
 
+    def ring_push(way, d, hops):
+        slot = ring_slot(way, d)
+        push(slot, slot, ring_send.at[way, d + hops], ring_recv.at[way, d + hops],
+             at_z(hops if way == 0 else depth - hops))
+
     def ring_step(s):
-        if s < right_steps:
-            if s >= 1:
-                arrived(ring_slot(z - s), ring_recv.at[0, s - 1])
-            push(ring_slot(z - s), ring_slot(z - s), ring_send.at[0, s],
-                 ring_recv.at[0, s], at_z(1))
-        if s < left_steps:
-            if s >= 1:
-                arrived(ring_slot(z + s), ring_recv.at[1, s - 1])
-            push(ring_slot(z + s), ring_slot(z + s), ring_send.at[1, s],
-                 ring_recv.at[1, s], at_z(depth - 1))
+        for way in range(2):
+            if s == 0:
+                ring_push(way, 0, 2)
+                ring_push(way, 0, 1)
+        for d in (2 * s - 1, 2 * s):
+            for way in range(2):
+                if 1 <= d <= reach[way]:
+                    arrived(ring_slot(way, d), ring_recv.at[way, d])
+                    if d + 2 <= reach[way]:
+                        ring_push(way, d, 2)
+
+    ring_steps = depth // 4
 
     ring_step(0)
 
@@ -150,7 +161,6 @@
     ss_y[0] = jnp.sum(ss_a[...], axis=0)
     exchange(ss_y, side, at_y, ss_send.at[1], ss_recv.at[1])
     ring_step(2)
-    ring_step(3)
     arrived(wrows.at[1 - core], w_recv)
     settle(ss_y, side, ss_recv.at[1])
     inverse = lax.rsqrt(jnp.sum(ss_y[...], axis=0) + EPS)
@@ -166,8 +176,7 @@
                            n1_send.at[0, d], n1_recv.at[0, d], at_x(d)))
         gather.append(push(normed.at[core, 1, :, y, x], normed.at[core, 1, :, y, x],
                            n1_send.at[1, d], n1_recv.at[1, d], at_y(d)))
-    ring_step(4)
-    ring_step(5)
+    ring_step(3)
     for d in range(1, side):
         px, py = lax.rem(x - d + side, side), lax.rem(y - d + side, side)
         arrived(normed.at[core, 0, :, y, px], n1_recv.at[0, d])
@@ -178,10 +187,8 @@
                                n2_send.at[0, c, d], n2_recv.at[0, c, d], at_y(d)))
             gather.append(push(normed.at[core, 1, c, :, x], normed.at[core, 1, c, :, x],
                                n2_send.at[1, c, d], n2_recv.at[1, c, d], at_x(d)))
-    for s in range(6, right_steps):
+    for s in range(4, ring_steps + 1):
         ring_step(s)
-    arrived(ring_slot(z - right_steps), ring_recv.at[0, right_steps - 1])
-    arrived(ring_slot(z + left_steps), ring_recv.at[1, left_steps - 1])
     features[...] = jnp.dot(onehot[...], gathered[...],
                             preferred_element_type=F32).astype(BF16)
 
@@ -200,10 +207,18 @@
             value = jnp.exp2(scores * factor)
             expo[:, target] = value
             total = jnp.sum(value.reshape(tokens // 8, 8, step_lanes), axis=0)
-            col_a[0, 0, pl.ds(row, 1), lanes] = jnp.sum(total, axis=0, keepdims=True)
+            col_a[0, which, 0, pl.ds(p * 2 + c, 1), lanes] = jnp.sum(total, axis=0, keepdims=True)
             return carry
 
         lax.fori_loop(0, 2 * (group // step_lanes), chunk, 0)
+
+    def pick(h, first, second):
+        return tuple(u * (1 - h) + v * h for u, v in zip(first, second))
+
+    def column_push(it, h):
+        for d in far_first(2 * side):
+            push(col_a.at[it, h, 0], col_a.at[it, h, d], a_send.at[it, h], a_recv.at[it, h],
+                 pick(h, at_q(d), at_qy(d)))
 
     for c in range(2):
         for d in range(1, side):
@@ -213,82 +228,87 @@
         gather.append(push(normed.at[core, :, c], normed.at[core, :, c],
                            share_send.at[c], share_recv.at[c], sibling))
         fill(core, c)
+    column_push(0, core)
     for c in range(2):
         arrived(normed.at[1 - core, :, c], share_recv.at[c])
         fill(1 - core, c)
-
-    def columns_to_scale(it):
-        exchange(col_a.at[it], 2 * side, at_q, a_send.at[it], a_recv.at[it])
-        settle(col_a.at[it], 2 * side, a_recv.at[it])
-        col_b[it, 0] = jnp.sum(col_a[it], axis=0)
-        exchange(col_b.at[it], side, at_y, b_send.at[it], b_recv.at[it])
-        settle(col_b.at[it], side, b_recv.at[it])
-        col_scale[...] = 1.0 / jnp.sum(col_b[it], axis=0)
-
-    def row_pass(it):
+    column_push(0, 1 - core)
+
+    def row_pass(h):
         def some(g, carry):
             here = pl.ds(pl.multiple_of(g * 64, 64), 64)
-            total = jnp.zeros((64, 128), F32)
-            for j in range(columns // 128):
+            total = jnp.zeros((64, 128), F32) if h == 0 else row_acc[here, :]
+            for j in range(half // 128):
                 k, l = j // (group // 128), j % (group // 128)
-                scale = col_scale[k:k + 1, 128 * l:128 * (l + 1)]
-                total += expo[here, 128 * j:128 * (j + 1)] * scale
+                scale = col_scale[h, k:k + 1, 128 * l:128 * (l + 1)]
+                lane = h * half + 128 * j
+                total += expo[here, lane:lane + 128] * scale
             row_acc[here, :] = total
             return carry
 
         lax.fori_loop(0, tokens // 64, some, 0)
+
+    def columns_to_rows(it):
+        for h in range(2):
+            settle(col_a.at[it, h], 2 * side, a_recv.at[it, h])
+            col_b[it, h, 0] = jnp.sum(col_a[it, h], axis=0)
+            exchange(col_b.at[it, h], side, (at_y, at_x)[h], b_send.at[it, h], b_recv.at[it, h])
+        for h in range(2):
+            settle(col_b.at[it, h], side, b_recv.at[it, h])
+            col_scale[h] = 1.0 / jnp.sum(col_b[it, h], axis=0)
+            row_pass(h)
         for j in range(tokens // 128):
             turned = row_acc[128 * j:128 * (j + 1), :].T
             row_x[it, 0, j:j + 1, :] = jnp.sum(turned, axis=0, keepdims=True)
+        exchange(row_x.at[it], depth, at_z, r_send.at[it], r_recv.at[it])
 
     def rows_to_scale(it):
-        exchange(row_x.at[it], depth, at_z, r_send.at[it], r_recv.at[it])
         settle(row_x.at[it], depth, r_recv.at[it])
         scale = 1.0 / jnp.sum(row_x[it], axis=0)
         for j in range(tokens // 128):
             row_bcast[128 * j:128 * (j + 1), :] = jnp.broadcast_to(
                 scale[j:j + 1, :], (128, 128)).T
 
-    def column_pass(it):
+    def column_pass(it, h):
         def chunk(k, carry):
-            target = pl.ds(pl.multiple_of(k * group, group), group)
-
+            target = pl.ds(pl.multiple_of(h * half + k * group, group), group)
             total = jnp.zeros((8, group), F32)
             for g in range(tokens // 64):
                 here = slice(g * 64, (g + 1) * 64)
                 scale = jnp.concatenate([row_bcast[here, :]] * (group // 128), axis=1)
                 value = expo[here, target] * scale
                 total += jnp.sum(value.reshape(8, 8, group), axis=0)
-            col_a[it, 0, pl.ds(k, 1), :] = jnp.sum(total, axis=0, keepdims=True)
+            col_a[it, h, 0, pl.ds(k, 1), :] = jnp.sum(total, axis=0, keepdims=True)
             return carry
 
-        lax.fori_loop(0, 8, chunk, 0)
+        lax.fori_loop(0, 4, chunk, 0)
 
     def sinkhorn(it, carry):
-        columns_to_scale(it)
-        row_pass(it)
+        columns_to_rows(it)
         rows_to_scale(it)
-        column_pass(it + 1)
+        for h in range(2):
+            column_pass(it + 1, h)
+            column_push(it + 1, h)
         return carry
 
     lax.fori_loop(0, ITERS - 1, sinkhorn, 0)
-    columns_to_scale(ITERS - 1)
-    row_pass(ITERS - 1)
-    rows_to_scale(ITERS - 1)
+    columns_to_rows(ITERS - 1)
 
     pltpu.make_async_copy(wrows.at[core], wrows.at[core], w_send).wait()
-    for s in range(right_steps):
-        arrived(ring_slot(z - s), ring_send.at[0, s])
-    for s in range(left_steps):
-        arrived(ring_slot(z + s), ring_send.at[1, s])
+    for way in range(2):
+        for d in range(1, reach[way] + 1):
+            arrived(ring_slot(way, d), ring_send.at[way, d])
     for copy in gather:
         copy.wait_send()
     settle(ss_a, 2 * side, ss_send.at[0])
     settle(ss_y, side, ss_send.at[1])
     for it in range(ITERS):
-        settle(col_a.at[it], 2 * side, a_send.at[it])
-        settle(col_b.at[it], side, b_send.at[it])
+        for h in range(2):
+            settle(col_a.at[it, h], 2 * side, a_send.at[it, h])
+            settle(col_b.at[it, h], side, b_send.at[it, h])
         settle(row_x.at[it], depth, r_send.at[it])
+
+    rows_to_scale(ITERS - 1)
 
 
 def finish_kernel(scale_out, expo, row_bcast, col_scale, out_ref, staged, sems):
@@ -302,7 +322,7 @@
         for k in range(8):
             target = slice(k * group, (k + 1) * group)
             value = scale_out * (expo[here, target] * scale)
-            staged[g, :, target] = (value * col_scale[k:k + 1, :]).astype(BF16)
+            staged[g, :, target] = (value * col_scale[k // 4, k % 4:k % 4 + 1, :]).astype(BF16)
         copies.append(pltpu.make_async_copy(staged.at[g], out_ref.at[pl.ds(g * step, step)],
                                             sems.at[g]))
         copies[-1].start()
@@ -323,7 +343,7 @@
         out_shape=(
             jax.ShapeDtypeStruct((tokens, columns), F32),
             jax.ShapeDtypeStruct((tokens, 128), F32),
-            jax.ShapeDtypeStruct((8, group), F32),
+            jax.ShapeDtypeStruct((2, 4, group), F32),
         ),
         in_specs=[hbm] * 3,
         out_specs=(vmem,) * 3,
@@ -340,18 +360,18 @@
             pltpu.VMEM((side, 8, half // 8), F32),
             pltpu.VMEM((2, 2, 2, side, side, 2 * rows, group), BF16),
             pltpu.VMEM((tokens, 128), F32),
-            pltpu.VMEM((ITERS, 2 * side, 8, group), F32),
-            pltpu.VMEM((ITERS, side, 8, group), F32),
+            pltpu.VMEM((ITERS, 2, 2 * side, 4, group), F32),
+            pltpu.VMEM((ITERS, 2, side, 4, group), F32),
             pltpu.VMEM((ITERS, depth, tokens // 128, 128), F32),
             dma((3,)),
-            dma((2, depth // 2)), dma((2, depth // 2)),
+            dma((2, depth // 2 + 1)), dma((2, depth // 2 + 1)),
             dma, dma,
             dma((2,)), dma((2,)),
             dma((2, side)), dma((2, side)),
             dma((2, 2, side)), dma((2, 2, side)),
             dma((2,)), dma((2,)),
-            dma((ITERS,)), dma((ITERS,)),
-            dma((ITERS,)), dma((ITERS,)),
+            dma((ITERS, 2)), dma((ITERS, 2)),
+            dma((ITERS, 2)), dma((ITERS, 2)),
             dma((ITERS,)), dma((ITERS,)),
         ],
         compiler_params=pltpu.CompilerParams(

time: 92.1 us -> 86.1 us (0.935)
  Pallas kernels: 91.8 us -> 86 us
    pallas_call x1, Pallas kernels: 89.6 us -> 83.8 us  [body(): pl.pallas_call(functools.partial(kernel, side, depth), out_shape=(jax.Sha...]
where the time goes in v2:
time: 86.1 us; the launch traced here: 86 us
  Pallas kernels  86 us (100%)
    pallas_call x1, Pallas kernels, body(): pl.pallas_call(functools.partial(kernel, side, depth), out_shape=(jax.Sha...  83.8 us
    pallas_call x1, Pallas kernels, body(): pl.pallas_call(functools.partial(finish_kernel, float(columns * depth)),...  2.19 us

profile of v2, /device:TPU:1, one launch (start us, length us, event | category | flops | bytes accessed | tf_op | source)
XLA Modules:
  0.0 86.0 jit_solution(1599291905699231834)
XLA Ops:
  0.0 83.8 %shard_map.37 = (f32[512,4096]{1,0:T(8,128)S(1)}, f32[512,128]{1,0:T(8,128)S(1)}, f32[2,4,512]{2,1,0:T(4,128)S(1)}) custom-call(bf16[64,256]{1,0:T(8,128)(2,1)} %patches_hbm.1, s32[4,128]{1,0:T(4,128)} %bitcast.1, f32[8,4096]{1,0:T(8,128)} %weight_hbm.1), custom_call_target="tpu_custom_call" | custom-call | flops 1073741824 | bytes 8388608 | tf_op jit(solution)/shard_map/pallas_call | solution.py:341
  83.8 2.2 %shard_map.38 = bf16[512,4096]{1,0:T(8,128)(2,1)} custom-call(f32[512,4096]{1,0:T(8,128)S(1)} %get-tuple-element.8.expo, f32[512,128]{1,0:T(8,128)S(1)} %get-tuple-element.9.row_bcast, f32[2,4,512]{2,1,0:T(4,128)S(1)} %get-tuple-element.10.col_scale), custom_call_target="tpu_custom_call" | custom-call | flops 6291456 | bytes 12582912 | tf_op jit(solution)/shard_map/pallas_call | solution.py:387

commit v3 on v2

--- a/solution.py
+++ b/solution.py
@@ -25,10 +25,10 @@
     patches_hbm, index_hbm, weight_hbm,
     expo, row_bcast, col_scale,
     patches_ref, index_ref, weight_ref,
-    gathered, onehot, features, wrows, ss_own, ss_a, ss_y, normed,
+    gathered, onehot, features, raw, ss_own, ss_a, ss_y, normed,
     row_acc, col_a, col_b, row_x,
-    load_sem, ring_send, ring_recv, w_send, w_recv, ss_send, ss_recv,
-    n1_send, n1_recv, n2_send, n2_recv, share_send, share_recv,
+    load_sem, ring_send, ring_recv, raw_send, raw_recv, ss_send, ss_recv,
+    n2_send, n2_recv, share_send, share_recv,
     a_send, a_recv, b_send, b_recv, r_send, r_recv,
 ):
     t = lax.axis_index("tok")
@@ -41,25 +41,25 @@
     sibling = (t + 1 - 2 * core, z)
     tokens, columns = expo.shape
     half = columns // 2
+    quarter = half // 2
     group = columns // 8
     part = half // 8
     block, width = patches_ref.shape
 
-    def at_z(d):
-        return (t, lax.rem(z + d, depth))
-
-    def at_q(d):
-        return (y * (2 * side) + lax.rem(q + d, 2 * side), z)
-
-    def at_qy(d):
-        to = lax.rem(y * 2 + core + d, 2 * side)
-        return ((to // 2) * (2 * side) + x * 2 + lax.rem(to, 2), z)
-
-    def at_x(d):
-        return ((y * side + lax.rem(x + d, side)) * 2 + core, z)
-
-    def at_y(d):
-        return (lax.rem(y + d, side) * (2 * side) + q, z)
+    def wrap(value, n):
+        return jnp.where(value >= n, value - n, value)
+
+    at_z, at_q, at_qy, at_x, at_y = {}, {}, {}, {}, {}
+    flip = (core, 1 - core)
+    for d in range(1, depth):
+        at_z[d] = (t, wrap(z + d, depth))
+    for d in range(1, 2 * side):
+        at_q[d] = (y * (2 * side) + wrap(q + d, 2 * side), z)
+        at_qy[d] = ((wrap(y * 2 + core + d, 2 * side) - flip[d % 2]) * side
+                    + x * 2 + flip[d % 2], z)
+    for d in range(1, side):
+        at_x[d] = ((y * side + wrap(x + d, side)) * 2 + core, z)
+        at_y[d] = (wrap(y + d, side) * (2 * side) + q, z)
 
     def push(src, dst, send, recv, device):
         copy = pltpu.make_async_remote_copy(
@@ -74,16 +74,15 @@
 
     def exchange(buf, n, device, send, recv):
         for d in far_first(n):
-            push(buf.at[0], buf.at[d], send, recv, device(d))
+            push(buf.at[0], buf.at[d], send, recv, device[d])
 
     def settle(buf, n, recv):
         arrived(buf.at[pl.ds(1, n - 1)], recv)
 
     barrier = pltpu.get_barrier_semaphore()
     partners = (
-        [at_z(1), at_z(2), at_z(depth - 1), at_z(depth - 2)]
-        + [at_q(d) for d in range(1, 2 * side)]
-        + [at_qy(d) for d in range(1, 2 * side)]
+        [at_z[d] for d in (1, 2, depth - 1, depth - 2)]
+        + list(at_q.values()) + list(at_qy.values())
     )
     for device in partners:
         pl.semaphore_signal(barrier, inc=1, device_id=device, device_id_type=MESH)
@@ -103,9 +102,11 @@
             lane = h * half + k * part
             ss_own[h, k:k + 1, :] = square[:, lane:lane + part]
     ss_a[0] = ss_own[core]
-    own_half = pl.ds(pl.multiple_of(core * half, half), half)
-    other_half = pl.ds(pl.multiple_of((1 - core) * half, half), half)
-    wrows[core] = weight_ref[:, own_half]
+    def quarter_of(h, p):
+        return pl.ds(pl.multiple_of(h * half + p * quarter, quarter), quarter)
+
+    raw[0, x, core] = weight_ref[:, quarter_of(core, 0)]
+    raw[1, y, core] = weight_ref[:, quarter_of(core, 1)]
 
     loads[1].wait()
     loads[2].wait()
@@ -117,18 +118,18 @@
     pl.semaphore_wait(barrier, len(partners))
 
     for d in far_first(2 * side):
-        push(ss_own.at[lax.rem(q + d, 2)], ss_a.at[d], ss_send.at[0], ss_recv.at[0], at_q(d))
+        push(ss_own.at[flip[d % 2]], ss_a.at[d], ss_send.at[0], ss_recv.at[0], at_q[d])
 
     reach = (depth // 2, depth - 1 - depth // 2)
 
     def ring_slot(way, d):
-        owner = lax.rem(z - d + depth, depth) if way == 0 else lax.rem(z + d, depth)
+        owner = wrap(z + (depth - d if way == 0 else d), depth)
         return gathered.at[pl.ds(pl.multiple_of(owner * block, block), block)]
 
     def ring_push(way, d, hops):
         slot = ring_slot(way, d)
         push(slot, slot, ring_send.at[way, d + hops], ring_recv.at[way, d + hops],
-             at_z(hops if way == 0 else depth - hops))
+             at_z[hops if way == 0 else depth - hops])
 
     def ring_step(s):
         for way in range(2):
@@ -146,7 +147,12 @@
 
     ring_step(0)
 
-    push(weight_ref.at[:, other_half], wrows.at[core], w_send, w_recv, sibling)
+    moves = []
+    for d in far_first(2 * side):
+        moves.append(push(weight_ref.at[:, quarter_of(flip[d % 2], 0)], raw.at[0, x, core],
+                          raw_send.at[0, d], raw_recv.at[0, d], at_q[d]))
+        moves.append(push(weight_ref.at[:, quarter_of(flip[d % 2], 1)], raw.at[1, y, core],
+                          raw_send.at[1, d], raw_recv.at[1, d], at_qy[d]))
 
     for j in range(tokens // 128):
         local = (index_ref[j:j + 1, :] - t * (block * depth)).astype(F32)
@@ -161,33 +167,29 @@
     ss_y[0] = jnp.sum(ss_a[...], axis=0)
     exchange(ss_y, side, at_y, ss_send.at[1], ss_recv.at[1])
     ring_step(2)
-    arrived(wrows.at[1 - core], w_recv)
+    for d in range(1, 2 * side):
+        px = wrap(q - d + 2 * side, 2 * side) // 2
+        py = wrap(y * 2 + core - d + 2 * side, 2 * side) // 2
+        arrived(raw.at[0, px, flip[d % 2]], raw_recv.at[0, d])
+        arrived(raw.at[1, py, flip[d % 2]], raw_recv.at[1, d])
     settle(ss_y, side, ss_recv.at[1])
     inverse = lax.rsqrt(jnp.sum(ss_y[...], axis=0) + EPS)
     for k in range(8):
-        value = wrows[:, :, k * part:(k + 1) * part].reshape(2 * wrows.shape[1], part)
-        lane = (k % 2) * part
-        normed[core, k // 4, (k // 2) % 2, y, x, :, lane:lane + part] = (
-            value * inverse[k:k + 1, :]).astype(BF16)
-
-    gather = []
-    for d in far_first(side):
-        gather.append(push(normed.at[core, 0, :, y, x], normed.at[core, 0, :, y, x],
-                           n1_send.at[0, d], n1_recv.at[0, d], at_x(d)))
-        gather.append(push(normed.at[core, 1, :, y, x], normed.at[core, 1, :, y, x],
-                           n1_send.at[1, d], n1_recv.at[1, d], at_y(d)))
-    ring_step(3)
-    for d in range(1, side):
-        px, py = lax.rem(x - d + side, side), lax.rem(y - d + side, side)
-        arrived(normed.at[core, 0, :, y, px], n1_recv.at[0, d])
-        arrived(normed.at[core, 1, :, py, x], n1_recv.at[1, d])
+        p, c, lane = k // 4, (k // 2) % 2, (k % 2) * part
+        value = raw[p, :, :, :, (k % 4) * part:(k % 4 + 1) * part].reshape(-1, part)
+        value = (value * inverse[k:k + 1, :]).astype(BF16).reshape(side, -1, part)
+        if p == 0:
+            normed[core, 0, c, y, :, :, lane:lane + part] = value
+        else:
+            normed[core, 1, c, :, x, :, lane:lane + part] = value
+
     for c in range(2):
         for d in far_first(side):
-            gather.append(push(normed.at[core, 0, c, y], normed.at[core, 0, c, y],
-                               n2_send.at[0, c, d], n2_recv.at[0, c, d], at_y(d)))
-            gather.append(push(normed.at[core, 1, c, :, x], normed.at[core, 1, c, :, x],
-                               n2_send.at[1, c, d], n2_recv.at[1, c, d], at_x(d)))
-    for s in range(4, ring_steps + 1):
+            moves.append(push(normed.at[core, 0, c, y], normed.at[core, 0, c, y],
+                              n2_send.at[0, c, d], n2_recv.at[0, c, d], at_y[d]))
+            moves.append(push(normed.at[core, 1, c, :, x], normed.at[core, 1, c, :, x],
+                              n2_send.at[1, c, d], n2_recv.at[1, c, d], at_x[d]))
+    for s in range(3, ring_steps + 1):
         ring_step(s)
     features[...] = jnp.dot(onehot[...], gathered[...],
                             preferred_element_type=F32).astype(BF16)
@@ -218,14 +220,14 @@
     def column_push(it, h):
         for d in far_first(2 * side):
             push(col_a.at[it, h, 0], col_a.at[it, h, d], a_send.at[it, h], a_recv.at[it, h],
-                 pick(h, at_q(d), at_qy(d)))
+                 pick(h, at_q[d], at_qy[d]))
 
     for c in range(2):
         for d in range(1, side):
-            px, py = lax.rem(x - d + side, side), lax.rem(y - d + side, side)
+            px, py = wrap(x - d + side, side), wrap(y - d + side, side)
             arrived(normed.at[core, 0, c, py], n2_recv.at[0, c, d])
             arrived(normed.at[core, 1, c, :, px], n2_recv.at[1, c, d])
-        gather.append(push(normed.at[core, :, c], normed.at[core, :, c],
+        moves.append(push(normed.at[core, :, c], normed.at[core, :, c],
                            share_send.at[c], share_recv.at[c], sibling))
         fill(core, c)
     column_push(0, core)
@@ -294,11 +296,10 @@
     lax.fori_loop(0, ITERS - 1, sinkhorn, 0)
     columns_to_rows(ITERS - 1)
 
-    pltpu.make_async_copy(wrows.at[core], wrows.at[core], w_send).wait()
     for way in range(2):
         for d in range(1, reach[way] + 1):
             arrived(ring_slot(way, d), ring_send.at[way, d])
-    for copy in gather:
+    for copy in moves:
         copy.wait_send()
     settle(ss_a, 2 * side, ss_send.at[0])
     settle(ss_y, side, ss_send.at[1])
@@ -354,7 +355,7 @@
             pltpu.VMEM((block * depth, width), BF16),
             pltpu.VMEM((tokens, block * depth), BF16),
             pltpu.VMEM((tokens, width), BF16),
-            pltpu.VMEM((2, rows, half), F32),
+            pltpu.VMEM((2, side, 2, rows, half // 2), F32),
             pltpu.VMEM((2, 8, half // 8), F32),
             pltpu.VMEM((2 * side, 8, half // 8), F32),
             pltpu.VMEM((side, 8, half // 8), F32),
@@ -365,9 +366,8 @@
             pltpu.VMEM((ITERS, depth, tokens // 128, 128), F32),
             dma((3,)),
             dma((2, depth // 2 + 1)), dma((2, depth // 2 + 1)),
-            dma, dma,
+            dma((2, 2 * side)), dma((2, 2 * side)),
             dma((2,)), dma((2,)),
-            dma((2, side)), dma((2, side)),
             dma((2, 2, side)), dma((2, 2, side)),
             dma((2,)), dma((2,)),
             dma((ITERS, 2)), dma((ITERS, 2)),

time: 86.1 us -> 84.3 us (0.979)
  Pallas kernels: 86 us -> 84.2 us
    pallas_call x1, Pallas kernels: 83.8 us -> 82 us  [body(): pl.pallas_call(functools.partial(kernel, side, depth), out_shape=(jax.Sha...]
where the time goes in v3:
time: 84.3 us; the launch traced here: 84.2 us
  Pallas kernels  84.2 us (100%)
    pallas_call x1, Pallas kernels, body(): pl.pallas_call(functools.partial(kernel, side, depth), out_shape=(jax.Sha...  82 us
    pallas_call x1, Pallas kernels, body(): pl.pallas_call(functools.partial(finish_kernel, float(columns * depth)),...  2.19 us

profile of v3, /device:TPU:1, one launch (start us, length us, event | category | flops | bytes accessed | tf_op | source)
XLA Modules:
  0.0 84.2 jit_solution(6579848315447868304)
XLA Ops:
  0.0 82.0 %shard_map.37 = (f32[512,4096]{1,0:T(8,128)S(1)}, f32[512,128]{1,0:T(8,128)S(1)}, f32[2,4,512]{2,1,0:T(4,128)S(1)}) custom-call(bf16[64,256]{1,0:T(8,128)(2,1)} %patches_hbm.1, s32[4,128]{1,0:T(4,128)} %bitcast.1, f32[8,4096]{1,0:T(8,128)} %weight_hbm.1), custom_call_target="tpu_custom_call" | custom-call | flops 1073741824 | bytes 8388608 | tf_op jit(solution)/shard_map/pallas_call | solution.py:342
  82.0 2.2 %shard_map.38 = bf16[512,4096]{1,0:T(8,128)(2,1)} custom-call(f32[512,4096]{1,0:T(8,128)S(1)} %get-tuple-element.8.expo, f32[512,128]{1,0:T(8,128)S(1)} %get-tuple-element.9.row_bcast, f32[2,4,512]{2,1,0:T(4,128)S(1)} %get-tuple-element.10.col_scale), custom_call_target="tpu_custom_call" | custom-call | flops 6291456 | bytes 12582912 | tf_op jit(solution)/shard_map/pallas_call | solution.py:387

commit v4 on v3

--- a/solution.py
+++ b/solution.py
@@ -79,6 +79,14 @@
     def settle(buf, n, recv):
         arrived(buf.at[pl.ds(1, n - 1)], recv)
 
+    loads = [
+        pltpu.make_async_copy(src, dst, load_sem.at[i])
+        for i, (src, dst) in enumerate((
+            (weight_hbm, weight_ref), (patches_hbm, patches_ref), (index_hbm, index_ref)))
+    ]
+    for load in loads:
+        load.start()
+
     barrier = pltpu.get_barrier_semaphore()
     partners = (
         [at_z[d] for d in (1, 2, depth - 1, depth - 2)]
@@ -87,14 +95,6 @@
     for device in partners:
         pl.semaphore_signal(barrier, inc=1, device_id=device, device_id_type=MESH)
 
-    loads = [
-        pltpu.make_async_copy(src, dst, load_sem.at[i])
-        for i, (src, dst) in enumerate((
-            (weight_hbm, weight_ref), (patches_hbm, patches_ref), (index_hbm, index_ref)))
-    ]
-    for load in loads:
-        load.start()
-
     loads[0].wait()
     square = jnp.sum(weight_ref[...] * weight_ref[...], axis=0, keepdims=True)
     for h in range(2):
@@ -102,6 +102,7 @@
             lane = h * half + k * part
             ss_own[h, k:k + 1, :] = square[:, lane:lane + part]
     ss_a[0] = ss_own[core]
+
     def quarter_of(h, p):
         return pl.ds(pl.multiple_of(h * half + p * quarter, quarter), quarter)
 
@@ -153,14 +154,6 @@
                           raw_send.at[0, d], raw_recv.at[0, d], at_q[d]))
         moves.append(push(weight_ref.at[:, quarter_of(flip[d % 2], 1)], raw.at[1, y, core],
                           raw_send.at[1, d], raw_recv.at[1, d], at_qy[d]))
-
-    for j in range(tokens // 128):
-        local = (index_ref[j:j + 1, :] - t * (block * depth)).astype(F32)
-        column = jnp.broadcast_to(local, (128, 128)).T
-        for k in range(block * depth // 128):
-            lane = lax.broadcasted_iota(jnp.int32, (128, 128), 1).astype(F32) + 128 * k
-            onehot[128 * j:128 * (j + 1), 128 * k:128 * (k + 1)] = jnp.where(
-                column == lane, 1.0, 0.0).astype(BF16)
 
     ring_step(1)
     settle(ss_a, 2 * side, ss_recv.at[0])
@@ -189,8 +182,19 @@
                               n2_send.at[0, c, d], n2_recv.at[0, c, d], at_y[d]))
             moves.append(push(normed.at[core, 1, c, :, x], normed.at[core, 1, c, :, x],
                               n2_send.at[1, c, d], n2_recv.at[1, c, d], at_x[d]))
-    for s in range(3, ring_steps + 1):
-        ring_step(s)
+        if c == 0:
+            for s in range(3, ring_steps):
+                ring_step(s)
+
+    for j in range(tokens // 128):
+        local = (index_ref[j:j + 1, :] - t * (block * depth)).astype(F32)
+        column = jnp.broadcast_to(local, (128, 128)).T
+        for k in range(block * depth // 128):
+            lane = lax.broadcasted_iota(jnp.int32, (128, 128), 1).astype(F32) + 128 * k
+            onehot[128 * j:128 * (j + 1), 128 * k:128 * (k + 1)] = jnp.where(
+                column == lane, 1.0, 0.0).astype(BF16)
+
+    ring_step(ring_steps)
     features[...] = jnp.dot(onehot[...], gathered[...],
                             preferred_element_type=F32).astype(BF16)
 
@@ -230,8 +234,8 @@
         moves.append(push(normed.at[core, :, c], normed.at[core, :, c],
                            share_send.at[c], share_recv.at[c], sibling))
         fill(core, c)
-    column_push(0, core)
-    for c in range(2):
+        if c == 1:
+            column_push(0, core)
         arrived(normed.at[1 - core, :, c], share_recv.at[c])
         fill(1 - core, c)
     column_push(0, 1 - core)
@@ -317,13 +321,14 @@
     group = columns // 8
     step = staged.shape[1]
     copies = []
+    col = scale_out * col_scale[...]
     for g in range(tokens // step):
         here = slice(g * step, (g + 1) * step)
         scale = jnp.concatenate([row_bcast[here, :]] * (group // 128), axis=1)
         for k in range(8):
             target = slice(k * group, (k + 1) * group)
-            value = scale_out * (expo[here, target] * scale)
-            staged[g, :, target] = (value * col_scale[k // 4, k % 4:k % 4 + 1, :]).astype(BF16)
+            value = (expo[here, target] * scale) * col[k // 4, k % 4:k % 4 + 1, :]
+            staged[g, :, target] = value.astype(BF16)
         copies.append(pltpu.make_async_copy(staged.at[g], out_ref.at[pl.ds(g * step, step)],
                                             sems.at[g]))
         copies[-1].start()

time: 84.3 us -> 85.3 us (1.012)
  Pallas kernels: 84.2 us -> 85.1 us
    pallas_call x1, Pallas kernels: 82 us -> 83 us  [body(): pl.pallas_call(functools.partial(kernel, side, depth), out_shape=(jax.Sha...]
where the time goes in v4:
time: 85.3 us; the launch traced here: 85.1 us
  Pallas kernels  85.1 us (100%)
    pallas_call x1, Pallas kernels, body(): pl.pallas_call(functools.partial(kernel, side, depth), out_shape=(jax.Sha...  83 us
    pallas_call x1, Pallas kernels, body(): pl.pallas_call(functools.partial(finish_kernel, float(columns * depth)),...  2.17 us

profile of v4, /device:TPU:1, one launch (start us, length us, event | category | flops | bytes accessed | tf_op | source)
XLA Modules:
  0.0 85.1 jit_solution(10594300127931087829)
XLA Ops:
  0.0 83.0 %shard_map.37 = (f32[512,4096]{1,0:T(8,128)S(1)}, f32[512,128]{1,0:T(8,128)S(1)}, f32[2,4,512]{2,1,0:T(4,128)S(1)}) custom-call(bf16[64,256]{1,0:T(8,128)(2,1)} %patches_hbm.1, s32[4,128]{1,0:T(4,128)} %bitcast.1, f32[8,4096]{1,0:T(8,128)} %weight_hbm.1), custom_call_target="tpu_custom_call" | custom-call | flops 1073741824 | bytes 8388608 | tf_op jit(solution)/shard_map/pallas_call | solution.py:347
  83.0 2.2 %shard_map.38 = bf16[512,4096]{1,0:T(8,128)(2,1)} custom-call(f32[512,4096]{1,0:T(8,128)S(1)} %get-tuple-element.8.expo, f32[512,128]{1,0:T(8,128)S(1)} %get-tuple-element.9.row_bcast, f32[2,4,512]{2,1,0:T(4,128)S(1)} %get-tuple-element.10.col_scale), custom_call_target="tpu_custom_call" | custom-call | flops 6291456 | bytes 12582912 | tf_op jit(solution)/shard_map/pallas_call | solution.py:392

commit v5 on v4

--- a/solution.py
+++ b/solution.py
@@ -26,10 +26,10 @@
     expo, row_bcast, col_scale,
     patches_ref, index_ref, weight_ref,
     gathered, onehot, features, raw, ss_own, ss_a, ss_y, normed,
-    row_acc, col_a, col_b, row_x,
+    row_acc, col_own, col_x, row_x,
     load_sem, ring_send, ring_recv, raw_send, raw_recv, ss_send, ss_recv,
     n2_send, n2_recv, share_send, share_recv,
-    a_send, a_recv, b_send, b_recv, r_send, r_recv,
+    a_send, a_recv, r_send, r_recv,
 ):
     t = lax.axis_index("tok")
     z = lax.axis_index("proto")
@@ -44,6 +44,8 @@
     quarter = half // 2
     group = columns // 8
     part = half // 8
+    step_lanes = columns // 16
+    plane = 2 * side * side
     block, width = patches_ref.shape
 
     def wrap(value, n):
@@ -60,6 +62,12 @@
     for d in range(1, side):
         at_x[d] = ((y * side + wrap(x + d, side)) * 2 + core, z)
         at_y[d] = (wrap(y + d, side) * (2 * side) + q, z)
+
+    at_plane = sorted(
+        ((min(dy, side - dy) + min(dq, 2 * side - dq) / 2, dy * 2 * side + dq,
+          (wrap(y + dy, side) * (2 * side) + wrap(q + dq, 2 * side), z))
+         for dy in range(side) for dq in range(2 * side) if dy + dq),
+        key=lambda item: (-item[0], item[1]))
 
     def push(src, dst, send, recv, device):
         copy = pltpu.make_async_remote_copy(
@@ -199,7 +207,6 @@
                             preferred_element_type=F32).astype(BF16)
 
     factor = math.log2(math.e) / TEMP
-    step_lanes = min(256, group)
 
     def fill(which, c):
         def chunk(i, carry):
@@ -207,24 +214,21 @@
             start = pl.multiple_of(lax.rem(i, group // step_lanes) * step_lanes, step_lanes)
             lanes = pl.ds(start, step_lanes)
             weights = normed[which, p, c, :, :, :, lanes].reshape(width, step_lanes)
-            row = which * 4 + p * 2 + c
-            target = pl.ds(pl.multiple_of(row * group + start, step_lanes), step_lanes)
+            row = (which * 4 + p * 2 + c) * (group // step_lanes) + start // step_lanes
+            target = pl.ds(pl.multiple_of(row * step_lanes, step_lanes), step_lanes)
             scores = jnp.dot(features[...], weights, preferred_element_type=F32)
             value = jnp.exp2(scores * factor)
             expo[:, target] = value
             total = jnp.sum(value.reshape(tokens // 8, 8, step_lanes), axis=0)
-            col_a[0, which, 0, pl.ds(p * 2 + c, 1), lanes] = jnp.sum(total, axis=0, keepdims=True)
+            col_own[pl.ds(row, 1), :] = jnp.sum(total, axis=0, keepdims=True)
             return carry
 
         lax.fori_loop(0, 2 * (group // step_lanes), chunk, 0)
 
-    def pick(h, first, second):
-        return tuple(u * (1 - h) + v * h for u, v in zip(first, second))
-
-    def column_push(it, h):
-        for d in far_first(2 * side):
-            push(col_a.at[it, h, 0], col_a.at[it, h, d], a_send.at[it, h], a_recv.at[it, h],
-                 pick(h, at_q[d], at_qy[d]))
+    def column_push(it):
+        col_x[it, 0] = col_own[...].astype(BF16)
+        for _, slot, device in at_plane:
+            push(col_x.at[it, 0], col_x.at[it, slot], a_send.at[it], a_recv.at[it], device)
 
     for c in range(2):
         for d in range(1, side):
@@ -232,37 +236,28 @@
             arrived(normed.at[core, 0, c, py], n2_recv.at[0, c, d])
             arrived(normed.at[core, 1, c, :, px], n2_recv.at[1, c, d])
         moves.append(push(normed.at[core, :, c], normed.at[core, :, c],
-                           share_send.at[c], share_recv.at[c], sibling))
+                          share_send.at[c], share_recv.at[c], sibling))
         fill(core, c)
-        if c == 1:
-            column_push(0, core)
+    for c in range(2):
         arrived(normed.at[1 - core, :, c], share_recv.at[c])
         fill(1 - core, c)
-    column_push(0, 1 - core)
-
-    def row_pass(h):
+    column_push(0)
+
+    def columns_to_rows(it):
+        settle(col_x.at[it], plane, a_recv.at[it])
+        col_scale[...] = 1.0 / jnp.sum(col_x[it].astype(F32), axis=0)
+
         def some(g, carry):
             here = pl.ds(pl.multiple_of(g * 64, 64), 64)
-            total = jnp.zeros((64, 128), F32) if h == 0 else row_acc[here, :]
-            for j in range(half // 128):
-                k, l = j // (group // 128), j % (group // 128)
-                scale = col_scale[h, k:k + 1, 128 * l:128 * (l + 1)]
-                lane = h * half + 128 * j
-                total += expo[here, lane:lane + 128] * scale
+            total = jnp.zeros((64, 128), F32)
+            for j in range(columns // 128):
+                k, l = j // (step_lanes // 128), j % (step_lanes // 128)
+                scale = col_scale[k:k + 1, 128 * l:128 * (l + 1)]
+                total += expo[here, 128 * j:128 * (j + 1)] * scale
             row_acc[here, :] = total
             return carry
 
         lax.fori_loop(0, tokens // 64, some, 0)
-
-    def columns_to_rows(it):
-        for h in range(2):
-            settle(col_a.at[it, h], 2 * side, a_recv.at[it, h])
-            col_b[it, h, 0] = jnp.sum(col_a[it, h], axis=0)
-            exchange(col_b.at[it, h], side, (at_y, at_x)[h], b_send.at[it, h], b_recv.at[it, h])
-        for h in range(2):
-            settle(col_b.at[it, h], side, b_recv.at[it, h])
-            col_scale[h] = 1.0 / jnp.sum(col_b[it, h], axis=0)
-            row_pass(h)
         for j in range(tokens // 128):
             turned = row_acc[128 * j:128 * (j + 1), :].T
             row_x[it, 0, j:j + 1, :] = jnp.sum(turned, axis=0, keepdims=True)
@@ -275,26 +270,28 @@
             row_bcast[128 * j:128 * (j + 1), :] = jnp.broadcast_to(
                 scale[j:j + 1, :], (128, 128)).T
 
-    def column_pass(it, h):
+    def column_pass():
         def chunk(k, carry):
-            target = pl.ds(pl.multiple_of(h * half + k * group, group), group)
+            target = pl.ds(pl.multiple_of(k * group, group), group)
             total = jnp.zeros((8, group), F32)
             for g in range(tokens // 64):
                 here = slice(g * 64, (g + 1) * 64)
                 scale = jnp.concatenate([row_bcast[here, :]] * (group // 128), axis=1)
                 value = expo[here, target] * scale
                 total += jnp.sum(value.reshape(8, 8, group), axis=0)
-            col_a[it, h, 0, pl.ds(k, 1), :] = jnp.sum(total, axis=0, keepdims=True)
+            total = jnp.sum(total, axis=0, keepdims=True)
+            for i in range(group // step_lanes):
+                col_own[pl.ds(k * (group // step_lanes) + i, 1), :] = (
+                    total[:, i * step_lanes:(i + 1) * step_lanes])
             return carry
 
-        lax.fori_loop(0, 4, chunk, 0)
+        lax.fori_loop(0, 8, chunk, 0)
 
     def sinkhorn(it, carry):
         columns_to_rows(it)
         rows_to_scale(it)
-        for h in range(2):
-            column_pass(it + 1, h)
-            column_push(it + 1, h)
+        column_pass()
+        column_push(it + 1)
         return carry
 
     lax.fori_loop(0, ITERS - 1, sinkhorn, 0)
@@ -308,9 +305,7 @@
     settle(ss_a, 2 * side, ss_send.at[0])
     settle(ss_y, side, ss_send.at[1])
     for it in range(ITERS):
-        for h in range(2):
-            settle(col_a.at[it, h], 2 * side, a_send.at[it, h])
-            settle(col_b.at[it, h], side, b_send.at[it, h])
+        settle(col_x.at[it], plane, a_send.at[it])
         settle(row_x.at[it], depth, r_send.at[it])
 
     rows_to_scale(ITERS - 1)
@@ -318,16 +313,16 @@
 
 def finish_kernel(scale_out, expo, row_bcast, col_scale, out_ref, staged, sems):
     tokens, columns = expo.shape
-    group = columns // 8
+    group = columns // 16
     step = staged.shape[1]
     copies = []
     col = scale_out * col_scale[...]
     for g in range(tokens // step):
         here = slice(g * step, (g + 1) * step)
         scale = jnp.concatenate([row_bcast[here, :]] * (group // 128), axis=1)
-        for k in range(8):
+        for k in range(16):
             target = slice(k * group, (k + 1) * group)
-            value = (expo[here, target] * scale) * col[k // 4, k % 4:k % 4 + 1, :]
+            value = (expo[here, target] * scale) * col[k:k + 1, :]
             staged[g, :, target] = value.astype(BF16)
         copies.append(pltpu.make_async_copy(staged.at[g], out_ref.at[pl.ds(g * step, step)],
                                             sems.at[g]))
@@ -349,7 +344,7 @@
         out_shape=(
             jax.ShapeDtypeStruct((tokens, columns), F32),
             jax.ShapeDtypeStruct((tokens, 128), F32),
-            jax.ShapeDtypeStruct((2, 4, group), F32),
+            jax.ShapeDtypeStruct((16, columns // 16), F32),
         ),
         in_specs=[hbm] * 3,
         out_specs=(vmem,) * 3,
@@ -366,8 +361,8 @@
             pltpu.VMEM((side, 8, half // 8), F32),
             pltpu.VMEM((2, 2, 2, side, side, 2 * rows, group), BF16),
             pltpu.VMEM((tokens, 128), F32),
-            pltpu.VMEM((ITERS, 2, 2 * side, 4, group), F32),
-            pltpu.VMEM((ITERS, 2, side, 4, group), F32),
+            pltpu.VMEM((16, columns // 16), F32),
+            pltpu.VMEM((ITERS, 2 * side * side, 16, columns // 16), BF16),
             pltpu.VMEM((ITERS, depth, tokens // 128, 128), F32),
             dma((3,)),
             dma((2, depth // 2 + 1)), dma((2, depth // 2 + 1)),
@@ -375,8 +370,7 @@
             dma((2,)), dma((2,)),
             dma((2, 2, side)), dma((2, 2, side)),
             dma((2,)), dma((2,)),
-            dma((ITERS, 2)), dma((ITERS, 2)),
-            dma((ITERS, 2)), dma((ITERS, 2)),
+            dma((ITERS,)), dma((ITERS,)),
             dma((ITERS,)), dma((ITERS,)),
         ],
         compiler_params=pltpu.CompilerParams(

time: 85.3 us -> 80.4 us (0.943)
  Pallas kernels: 85.1 us -> 80.3 us
    pallas_call x1, Pallas kernels: 83 us -> 78.1 us  [body(): pl.pallas_call(functools.partial(kernel, side, depth), out_shape=(jax.Sha...]
where the time goes in v5:
time: 80.4 us; the launch traced here: 80.3 us
  Pallas kernels  80.3 us (100%)
    pallas_call x1, Pallas kernels, body(): pl.pallas_call(functools.partial(kernel, side, depth), out_shape=(jax.Sha...  78.1 us
    pallas_call x1, Pallas kernels, body(): pl.pallas_call(functools.partial(finish_kernel, float(columns * depth)),...  2.16 us

profile of v5, /device:TPU:1, one launch (start us, length us, event | category | flops | bytes accessed | tf_op | source)
XLA Modules:
  0.0 80.3 jit_solution(11814755054158957843)
XLA Ops:
  0.0 78.1 %shard_map.37 = (f32[512,4096]{1,0:T(8,128)S(1)}, f32[512,128]{1,0:T(8,128)S(1)}, f32[16,256]{1,0:T(8,128)S(1)}) custom-call(bf16[64,256]{1,0:T(8,128)(2,1)} %patches_hbm.1, s32[4,128]{1,0:T(4,128)} %bitcast.1, f32[8,4096]{1,0:T(8,128)} %weight_hbm.1), custom_call_target="tpu_custom_call" | custom-call | flops 1073741824 | bytes 8388608 | tf_op jit(solution)/shard_map/pallas_call | solution.py:342
  78.2 2.2 %shard_map.38 = bf16[512,4096]{1,0:T(8,128)(2,1)} custom-call(f32[512,4096]{1,0:T(8,128)S(1)} %get-tuple-element.8.expo, f32[512,128]{1,0:T(8,128)S(1)} %get-tuple-element.9.row_bcast, f32[16,256]{1,0:T(8,128)S(1)} %get-tuple-element.10.col_scale), custom_call_target="tpu_custom_call" | custom-call | flops 6291456 | bytes 12582912 | tf_op jit(solution)/shard_map/pallas_call | solution.py:386

commit v6 on v5

--- a/solution.py
+++ b/solution.py
@@ -23,10 +23,10 @@
 def kernel(
     side, depth,
     patches_hbm, index_hbm, weight_hbm,
-    expo, row_bcast, col_scale,
+    expo, row_bcast,
     patches_ref, index_ref, weight_ref,
     gathered, onehot, features, raw, ss_own, ss_a, ss_y, normed,
-    row_acc, col_own, col_x, row_x,
+    row_acc, col_own, col_scale, col_x, row_x,
     load_sem, ring_send, ring_recv, raw_send, raw_recv, ss_send, ss_recv,
     n2_send, n2_recv, share_send, share_recv,
     a_send, a_recv, r_send, r_recv,
@@ -243,7 +243,7 @@
         fill(1 - core, c)
     column_push(0)
 
-    def columns_to_rows(it):
+    def columns_to_rows(it, last=False):
         settle(col_x.at[it], plane, a_recv.at[it])
         col_scale[...] = 1.0 / jnp.sum(col_x[it].astype(F32), axis=0)
 
@@ -253,7 +253,10 @@
             for j in range(columns // 128):
                 k, l = j // (step_lanes // 128), j % (step_lanes // 128)
                 scale = col_scale[k:k + 1, 128 * l:128 * (l + 1)]
-                total += expo[here, 128 * j:128 * (j + 1)] * scale
+                value = expo[here, 128 * j:128 * (j + 1)] * scale
+                total += value
+                if last:
+                    expo[here, 128 * j:128 * (j + 1)] = value
             row_acc[here, :] = total
             return carry
 
@@ -295,7 +298,7 @@
         return carry
 
     lax.fori_loop(0, ITERS - 1, sinkhorn, 0)
-    columns_to_rows(ITERS - 1)
+    columns_to_rows(ITERS - 1, last=True)
 
     for way in range(2):
         for d in range(1, reach[way] + 1):
@@ -311,19 +314,17 @@
     rows_to_scale(ITERS - 1)
 
 
-def finish_kernel(scale_out, expo, row_bcast, col_scale, out_ref, staged, sems):
+def finish_kernel(scale_out, expo, row_bcast, out_ref, staged, sems):
     tokens, columns = expo.shape
-    group = columns // 16
+    group = columns // 8
     step = staged.shape[1]
     copies = []
-    col = scale_out * col_scale[...]
     for g in range(tokens // step):
         here = slice(g * step, (g + 1) * step)
-        scale = jnp.concatenate([row_bcast[here, :]] * (group // 128), axis=1)
-        for k in range(16):
+        scale = jnp.concatenate([scale_out * row_bcast[here, :]] * (group // 128), axis=1)
+        for k in range(8):
             target = slice(k * group, (k + 1) * group)
-            value = (expo[here, target] * scale) * col[k:k + 1, :]
-            staged[g, :, target] = value.astype(BF16)
+            staged[g, :, target] = (expo[here, target] * scale).astype(BF16)
         copies.append(pltpu.make_async_copy(staged.at[g], out_ref.at[pl.ds(g * step, step)],
                                             sems.at[g]))
         copies[-1].start()
@@ -339,15 +340,14 @@
     dma = pltpu.SemaphoreType.DMA
     vmem = pl.BlockSpec(memory_space=pltpu.VMEM)
     hbm = pl.BlockSpec(memory_space=pltpu.HBM)
-    expo, row_bcast, col_scale = pl.pallas_call(
+    expo, row_bcast = pl.pallas_call(
         functools.partial(kernel, side, depth),
         out_shape=(
             jax.ShapeDtypeStruct((tokens, columns), F32),
             jax.ShapeDtypeStruct((tokens, 128), F32),
-            jax.ShapeDtypeStruct((16, columns // 16), F32),
         ),
         in_specs=[hbm] * 3,
-        out_specs=(vmem,) * 3,
+        out_specs=(vmem,) * 2,
         scratch_shapes=[
             pltpu.VMEM((block, width), BF16),
             pltpu.VMEM((tokens // 128, 128), jnp.int32),
@@ -361,6 +361,7 @@
             pltpu.VMEM((side, 8, half // 8), F32),
             pltpu.VMEM((2, 2, 2, side, side, 2 * rows, group), BF16),
             pltpu.VMEM((tokens, 128), F32),
+            pltpu.VMEM((16, columns // 16), F32),
             pltpu.VMEM((16, columns // 16), F32),
             pltpu.VMEM((ITERS, 2 * side * side, 16, columns // 16), BF16),
             pltpu.VMEM((ITERS, depth, tokens // 128, 128), F32),
@@ -382,18 +383,18 @@
             transcendentals=tokens * columns),
     )(*(pltpu.with_memory_space_constraint(v, pltpu.HBM) for v in (
         patches, mask_index.reshape(tokens // 128, 128), proto_weight)))
-    step = 64
+    step = 32
     return pl.pallas_call(
         functools.partial(finish_kernel, float(columns * depth)),
         out_shape=jax.ShapeDtypeStruct((tokens, columns), BF16),
-        in_specs=[vmem] * 3,
+        in_specs=[vmem] * 2,
         out_specs=hbm,
         scratch_shapes=[pltpu.VMEM((tokens // step, step, columns), BF16),
                         dma((tokens // step,))],
         compiler_params=pltpu.CompilerParams(vmem_limit_bytes=16 * 1024 * 1024),
         cost_estimate=pl.CostEstimate(
             flops=3 * tokens * columns, bytes_accessed=6 * tokens * columns, transcendentals=0),
-    )(expo, row_bcast, col_scale)
+    )(expo, row_bcast)
 
 
 def solution(mesh):

time: 80.4 us -> 80.5 us (level)
  no operation moved by 1% of the time
where the time goes in v6:
time: 80.5 us; the launch traced here: 80.3 us
  Pallas kernels  80.3 us (100%)
    pallas_call x1, Pallas kernels, body(): pl.pallas_call(functools.partial(kernel, side, depth), out_shape=(jax.Sha...  78.2 us
    pallas_call x1, Pallas kernels, body(): pl.pallas_call(functools.partial(finish_kernel, float(columns * depth)),...  2.17 us

profile of v6, /device:TPU:1, one launch (start us, length us, event | category | flops | bytes accessed | tf_op | source)
XLA Modules:
  0.0 80.3 jit_solution(1044948239060687588)
XLA Ops:
  0.0 78.2 %shard_map.37 = (f32[512,4096]{1,0:T(8,128)S(1)}, f32[512,128]{1,0:T(8,128)S(1)}) custom-call(bf16[64,256]{1,0:T(8,128)(2,1)} %patches_hbm.1, s32[4,128]{1,0:T(4,128)} %bitcast.1, f32[8,4096]{1,0:T(8,128)} %weight_hbm.1), custom_call_target="tpu_custom_call" | custom-call | flops 1073741824 | bytes 8388608 | tf_op jit(solution)/shard_map/pallas_call | solution.py:343
  78.2 2.2 %shard_map.38 = bf16[512,4096]{1,0:T(8,128)(2,1)} custom-call(f32[512,4096]{1,0:T(8,128)S(1)} %get-tuple-element.7.expo, f32[512,128]{1,0:T(8,128)S(1)} %get-tuple-element.8.row_bcast), custom_call_target="tpu_custom_call" | custom-call | flops 6291456 | bytes 12582912 | tf_op jit(solution)/shard_map/pallas_call | solution.py:387

commit v7 on v6

--- a/solution.py
+++ b/solution.py
@@ -231,15 +231,19 @@
             push(col_x.at[it, 0], col_x.at[it, slot], a_send.at[it], a_recv.at[it], device)
 
     for c in range(2):
-        for d in range(1, side):
-            px, py = wrap(x - d + side, side), wrap(y - d + side, side)
-            arrived(normed.at[core, 0, c, py], n2_recv.at[0, c, d])
-            arrived(normed.at[core, 1, c, :, px], n2_recv.at[1, c, d])
-        moves.append(push(normed.at[core, :, c], normed.at[core, :, c],
-                          share_send.at[c], share_recv.at[c], sibling))
+        for p in range(2):
+            for d in range(1, side):
+                if p == 0:
+                    block_ref = normed.at[core, 0, c, wrap(y - d + side, side)]
+                else:
+                    block_ref = normed.at[core, 1, c, :, wrap(x - d + side, side)]
+                arrived(block_ref, n2_recv.at[p, c, d])
+            moves.append(push(normed.at[core, p, c], normed.at[core, p, c],
+                              share_send.at[p, c], share_recv.at[p, c], sibling))
         fill(core, c)
     for c in range(2):
-        arrived(normed.at[1 - core, :, c], share_recv.at[c])
+        for p in range(2):
+            arrived(normed.at[1 - core, p, c], share_recv.at[p, c])
         fill(1 - core, c)
     column_push(0)
 
@@ -327,7 +331,7 @@
             staged[g, :, target] = (expo[here, target] * scale).astype(BF16)
         copies.append(pltpu.make_async_copy(staged.at[g], out_ref.at[pl.ds(g * step, step)],
                                             sems.at[g]))
-        copies[-1].start()
+        copies[-1].start(priority=g % 2)
     for copy in copies:
         copy.wait()
 
@@ -370,7 +374,7 @@
             dma((2, 2 * side)), dma((2, 2 * side)),
             dma((2,)), dma((2,)),
             dma((2, 2, side)), dma((2, 2, side)),
-            dma((2,)), dma((2,)),
+            dma((2, 2)), dma((2, 2)),
             dma((ITERS,)), dma((ITERS,)),
             dma((ITERS,)), dma((ITERS,)),
         ],

time: 80.5 us -> 80.8 us (level)
  no operation moved by 1% of the time
where the time goes in v7:
time: 80.8 us; the launch traced here: 80.7 us
  Pallas kernels  80.7 us (100%)
    pallas_call x1, Pallas kernels, body(): pl.pallas_call(functools.partial(kernel, side, depth), out_shape=(jax.Sha...  78.5 us
    pallas_call x1, Pallas kernels, body(): pl.pallas_call(functools.partial(finish_kernel, float(columns * depth)),...  2.17 us

profile of v7, /device:TPU:1, one launch (start us, length us, event | category | flops | bytes accessed | tf_op | source)
XLA Modules:
  0.0 80.7 jit_solution(18398718517287916143)
XLA Ops:
  0.0 78.5 %shard_map.37 = (f32[512,4096]{1,0:T(8,128)S(1)}, f32[512,128]{1,0:T(8,128)S(1)}) custom-call(bf16[64,256]{1,0:T(8,128)(2,1)} %patches_hbm.1, s32[4,128]{1,0:T(4,128)} %bitcast.1, f32[8,4096]{1,0:T(8,128)} %weight_hbm.1), custom_call_target="tpu_custom_call" | custom-call | flops 1073741824 | bytes 8388608 | tf_op jit(solution)/shard_map/pallas_call | solution.py:347
  78.5 2.2 %shard_map.38 = bf16[512,4096]{1,0:T(8,128)(2,1)} custom-call(f32[512,4096]{1,0:T(8,128)S(1)} %get-tuple-element.7.expo, f32[512,128]{1,0:T(8,128)S(1)} %get-tuple-element.8.row_bcast), custom_call_target="tpu_custom_call" | custom-call | flops 6291456 | bytes 12582912 | tf_op jit(solution)/shard_map/pallas_call | solution.py:391
